TPU v7x, 32 devices: a whole 2x2x4 slice. The times are simulated.
32 devices in a mesh: seq: 8 (over z, core), mp: 4 (over y, x).
Axes of the slice: x: 2, y: 2, z: 4, core: 2. Of those that a mesh axis runs over, the one named last changes fastest.
Arguments:
- qkv_owned: bfloat16 [4, 3072, 6144], P('mp', 'seq'), may hold values from -6 to 6, as said below
- owner: int32 [4, 1024], P('mp'), may hold values from 0 to 7, as said below
- band_rows: int32 [4, 8, 4], P('mp'), may hold values from 0 to 7, as said below
- band_cols: int32 [4, 8, 4], P('mp'), may hold values from 0 to 7
- bias: float32 [16, 2], replicated, may hold values from -1.5 to 1.5
- grad_out: bfloat16 [4, 1024, 2048], P('mp', 'seq'), may hold values from -6 to 6
Outputs:
- attended: bfloat16 [4, 1024, 2048], P('mp', 'seq')
- grad_qkv: bfloat16 [4, 3072, 6144], P('mp', 'seq')
- grad_bias: float32 [16, 2], P('seq')
Inputs may be any that keep to these rules, and one draw needn't show every extreme that they name: Within the 128 positions p * 128 to p * 128 + 127 of a document, at most 48 name one owner, and in every such shard some owner is named exactly 48 times. band_rows[b, 0] is b; the 8 blocks of band_rows[b] and band_cols[b] are distinct. `qkv_owned`: rows that no position names are not read.
All inputs are finite; a program needn't handle non-finite values.
Results may differ from a plain program's by a relative error of at most 0.04.
Values may be sent and summed in bfloat16 or wider, within the bound.
A program may use at most 128 MiB of HBM per device.

v0:
```python
import math

import jax
import jax.numpy as jnp
from jax import lax
from jax.sharding import PartitionSpec as P

HEADS = 16
HEAD_DIM = 128
ROW_BLOCKS = 4


def owner_tables(owner_all, num_dev, tok_rows):
    owner_ids = jnp.arange(num_dev, dtype=jnp.int32)
    onehot = (owner_all[:, None] == owner_ids[None, :]).astype(jnp.int32)
    running = jnp.cumsum(onehot, axis=0) - onehot
    slot_index = jnp.sum(running * onehot, axis=1)
    per_shard = jnp.sum(onehot.reshape(num_dev, tok_rows, num_dev), axis=1)
    return (onehot, slot_index, per_shard)


def attend_both(head_rows, grad_heads, selected, bias_pair, row_count):
    length, _, per_dev, head_dim = head_rows.shape
    num_blocks, num_sel = selected.shape
    blk_rows = length // num_blocks
    score_scaling = 1.0 / math.sqrt(head_dim)

    def blocks(array):
        return array.reshape(num_blocks, blk_rows, per_dev, head_dim).transpose(2, 0, 1, 3)

    def unblock(array):
        return array.transpose(1, 2, 0, 3).reshape(length, per_dev * head_dim)

    query_tile_block = blocks(head_rows[:, 0])
    key_block = blocks(head_rows[:, 1])
    value_block = blocks(head_rows[:, 2])
    gradient_per_block = blocks(grad_heads)
    selected_keys = key_block[:, selected].reshape(
        per_dev, num_blocks, num_sel * blk_rows, head_dim
    )
    selected_values = value_block[:, selected].reshape(
        per_dev, num_blocks, num_sel * blk_rows, head_dim
    )
    col_kind = jnp.arange(num_sel * blk_rows) >= row_count * blk_rows
    key_offset_bias = jnp.where(col_kind[None, :], bias_pair[:, 1:2], bias_pair[:, 0:1])
    logit_scores = (
        jnp.einsum(
            "hbqd,hbkd->hbqk", query_tile_block, selected_keys, preferred_element_type=jnp.float32
        )
        * score_scaling
    )
    logit_scores = logit_scores + key_offset_bias[:, None, None, :]
    row_max = jnp.max(logit_scores, axis=-1, keepdims=True)
    exp_scores = jnp.exp(logit_scores - row_max)
    weights = exp_scores / jnp.sum(exp_scores, axis=-1, keepdims=True)
    reduced_weights = weights.astype(jnp.bfloat16)
    attention_result = jnp.einsum(
        "hbqk,hbkd->hbqd", reduced_weights, selected_values, preferred_element_type=jnp.float32
    ).astype(jnp.bfloat16)
    row_delta = jnp.sum(
        gradient_per_block.astype(jnp.float32) * attention_result.astype(jnp.float32),
        axis=-1,
        keepdims=True,
    )
    probability_gradient = jnp.einsum(
        "hbqd,hbkd->hbqk", gradient_per_block, selected_values, preferred_element_type=jnp.float32
    )
    dscore = weights * (probability_gradient - row_delta)
    bias_grad = jnp.stack(
        [
            jnp.sum(jnp.where(col_kind, 0.0, dscore), axis=(1, 2, 3)),
            jnp.sum(jnp.where(col_kind, dscore, 0.0), axis=(1, 2, 3)),
        ],
        axis=1,
    )
    score_gradient_reduced = dscore.astype(jnp.bfloat16)
    query_gradient = (
        jnp.einsum(
            "hbqk,hbkd->hbqd",
            score_gradient_reduced,
            selected_keys,
            preferred_element_type=jnp.float32,
        )
        * score_scaling
    )
    selected_key_gradient = (
        jnp.einsum(
            "hbqk,hbqd->hbkd",
            score_gradient_reduced,
            query_tile_block,
            preferred_element_type=jnp.float32,
        )
        * score_scaling
    )
    selected_value_gradient = jnp.einsum(
        "hbqk,hbqd->hbkd", reduced_weights, gradient_per_block, preferred_element_type=jnp.float32
    )
    block_hot = (
        selected[:, :, None] == jnp.arange(num_blocks, dtype=jnp.int32)[None, None, :]
    ).astype(jnp.float32)
    grad_key = jnp.einsum(
        "bjc,hbjtd->hctd",
        block_hot,
        selected_key_gradient.reshape(per_dev, num_blocks, num_sel, blk_rows, head_dim),
        precision=lax.Precision.HIGHEST,
    )
    grad_value = jnp.einsum(
        "bjc,hbjtd->hctd",
        block_hot,
        selected_value_gradient.reshape(per_dev, num_blocks, num_sel, blk_rows, head_dim),
        precision=lax.Precision.HIGHEST,
    )
    return (
        unblock(attention_result),
        unblock(query_gradient),
        unblock(grad_key),
        unblock(grad_value),
        bias_grad,
    )


def shards(qkv_owned, owner, band_rows, band_cols, bias, grad_out):
    num_dev = lax.axis_size("seq")
    my_index = lax.axis_index("seq")
    slot_count = qkv_owned.shape[1]
    features = qkv_owned.shape[2]
    tok_rows = grad_out.shape[1]
    row_width = grad_out.shape[2]
    per_dev = HEADS // num_dev
    group_width = per_dev * HEAD_DIM
    capacity = slot_count // num_dev
    length = tok_rows * num_dev
    owner_all = owner[0]
    onehot, slot_index, per_shard = owner_tables(owner_all, num_dev, tok_rows)
    selected = jnp.concatenate([band_rows[0], band_cols[0]], axis=1)
    bias_pair = lax.dynamic_slice_in_dim(bias, my_index * per_dev, per_dev, 0)
    cell_rows = qkv_owned[0]
    before = jnp.cumsum(per_shard, axis=0) - per_shard
    counts = lax.dynamic_index_in_dim(per_shard, my_index, 1, False)
    starts = lax.dynamic_index_in_dim(before, my_index, 1, False)
    within = jnp.arange(capacity, dtype=jnp.int32)
    pick_rows = jnp.minimum(starts[:, None] + within[None, :], slot_count - 1).reshape(
        num_dev * capacity
    )
    outgoing = jnp.take(cell_rows, pick_rows, axis=0)
    arrived = lax.all_to_all(outgoing, "seq", split_axis=0, concat_axis=0, tiled=True)
    mine_hot = lax.dynamic_slice_in_dim(onehot, my_index * tok_rows, tok_rows, 0)
    slot_mine = lax.dynamic_slice_in_dim(slot_index, my_index * tok_rows, tok_rows, 0)
    owner_mine = lax.dynamic_slice_in_dim(owner_all, my_index * tok_rows, tok_rows, 0)
    before_mine = lax.dynamic_index_in_dim(before, my_index, 0, False)
    base_mine = jnp.sum(mine_hot * before_mine[None, :], axis=1)
    local_rows = owner_mine * capacity + slot_mine - base_mine
    balanced = jnp.take(arrived, local_rows, axis=0).reshape(tok_rows, 3, num_dev, group_width)
    grad_parts = grad_out[0].reshape(tok_rows, 1, num_dev, group_width)
    head_rows, grad_heads = (
        lax.all_to_all(balanced, "seq", split_axis=2, concat_axis=0, tiled=True),
        lax.all_to_all(grad_parts, "seq", split_axis=2, concat_axis=0, tiled=True),
    )
    head_rows = head_rows.reshape(length, 3, per_dev, HEAD_DIM)
    grad_heads = grad_heads.reshape(length, per_dev, HEAD_DIM)
    attention_result, query_gradient, grad_key, grad_value, bias_grad = attend_both(
        head_rows, grad_heads, selected, bias_pair, ROW_BLOCKS
    )
    grad_rows = jnp.stack([query_gradient, grad_key, grad_value], axis=1).astype(jnp.bfloat16)
    out_rows, grad_back = (
        lax.all_to_all(
            attention_result.reshape(length, 1, group_width),
            "seq",
            split_axis=0,
            concat_axis=2,
            tiled=True,
        ),
        lax.all_to_all(grad_rows, "seq", split_axis=0, concat_axis=2, tiled=True),
    )
    send_back = (
        jnp.zeros((num_dev * capacity, features), jnp.bfloat16)
        .at[local_rows]
        .set(grad_back.reshape(tok_rows, features))
    )
    returned = lax.all_to_all(send_back, "seq", split_axis=0, concat_axis=0, tiled=True)
    target = jnp.where(
        within[None, :] < counts[:, None], starts[:, None] + within[None, :], slot_count
    ).reshape(num_dev * capacity)
    grad_cells = (
        jnp.zeros((slot_count + 1, features), jnp.bfloat16).at[target].set(returned)[:slot_count]
    )
    attended_rows = out_rows.reshape(tok_rows, row_width)
    bias_total = lax.psum(bias_grad, "mp")
    return (
        attended_rows.reshape(1, tok_rows, row_width),
        grad_cells.reshape(1, slot_count, features),
        bias_total,
    )


def solution(mesh):
    in_specs = (
        P("mp", "seq", None),
        P("mp", None),
        P("mp", None, None),
        P("mp", None, None),
        P(),
        P("mp", "seq", None),
    )
    out_specs = (P("mp", "seq", None), P("mp", "seq", None), P("seq", None))
    return jax.shard_map(shards, mesh=mesh, in_specs=in_specs, out_specs=out_specs, check_vma=False)
```

profile of v0, /device:TPU:0, one launch (start us, length us, event | category | flops | bytes accessed | tf_op | source)
XLA Modules:
  0.0 471.6 jit_solution(11247210034039990835)
XLA Ops:
  2.1 14.6 %gather_fusion = bf16[384,6144]{1,0:T(8,128)(2,1)} fusion(bf16[384,6144]{1,0:T(8,128)(2,1)} %bitcast.152, s32[1024]{0:T(1024)S(1)} %pad_clamp_fusion.2), kind=kCustom, calls=%fused_computation | custom fusion | bytes 9438720 | tf_op jit(solution)/shard_map/jit(_take)/gather | solution.py:145
  16.7 5.0 %broadcast_select_fusion = bf16[8,48,6144]{2,1,0:T(8,128)(2,1)} fusion(bf16[8,48,6144]{2,1,0:T(8,128)(2,1)} %bitcast.158, pred[8,48]{1,0:T(8,128)(4,1)S(1)} %compare_and_fusion), kind=kLoop, calls=%fused_computation.18 | loop fusion | flops 2359296 | bytes 9437568 | tf_op jit(solution)/shard_map/jit(_take)/select_n | solution.py:145
  21.7 6.5 %all-to-all-start = ((bf16[8,48,6144]{2,1,0:T(8,128)(2,1)}), bf16[8,48,6144]{2,1,0:T(8,128)(2,1)}, u32[]{:S(2)}, u32[]{:S(2)}) async-start(bf16[8,48,6144]{2,1,0:T(8,128)(2,1)} %broadcast_select_fusion), calls=%async_computation | async-start | bytes 9437184 | tf_op jit(solution)/shard_map/all_to_all | solution.py:146
  31.2 102.3 %all-to-all-done = bf16[8,48,6144]{2,1,0:T(8,128)(2,1)} async-done(((bf16[8,48,6144]{2,1,0:T(8,128)(2,1)}), bf16[8,48,6144]{2,1,0:T(8,128)(2,1)}, u32[]{:S(2)}, u32[]{:S(2)}) %all-to-all-start) | async-done | bytes 4718624 | tf_op jit(solution)/shard_map/all_to_all | solution.py:146
  133.5 5.9 %gather_fusion.1 = bf16[128,6144]{1,0:T(8,128)(2,1)S(1)} fusion(bf16[384,6144]{1,0:T(8,128)(2,1)} %bitcast.7, s32[1024]{0:T(1024)S(1)} %pad_clamp_fusion.1), kind=kCustom, calls=%fused_computation.1 | custom fusion | bytes 3146240 | tf_op jit(solution)/shard_map/jit(_take)/gather | solution.py:153
  148.8 35.3 %all-to-all-done.1 = bf16[128,3,8,256]{0,3,1,2:T(8,128)(2,1)S(1)} async-done(((bf16[128,3,8,256]{0,3,1,2:T(8,128)(2,1)}), bf16[128,3,8,256]{0,3,1,2:T(8,128)(2,1)S(1)}, u32[]{:S(2)}, u32[]{:S(2)}) %all-to-all-start.1) | async-done | bytes 1572896 | tf_op jit(solution)/shard_map/all_to_all | solution.py:156
  195.3 4.7 %copy.169 = bf16[2,8,8,128,128]{4,3,2,1,0:T(8,128)(2,1)} copy(bf16[2,8,8,128,128]{4,3,0,2,1:T(8,128)(2,1)} %bitcast.164) | data formatting | bytes 8388608 | tf_op jit(solution)/shard_map/gather | solution.py:38
  203.7 4.7 %copy.171 = bf16[2,8,8,128,128]{4,3,2,1,0:T(8,128)(2,1)} copy(bf16[2,8,8,128,128]{4,3,0,2,1:T(8,128)(2,1)} %bitcast.163) | data formatting | bytes 8388608 | tf_op jit(solution)/shard_map/gather | solution.py:41
  208.5 8.1 %fusion.69 = (f32[2,8,128]{2,1,0:T(8,128)S(1)}, f32[2,8,128,1024]{3,2,1,0:T(8,128)}) fusion(f32[2,1024]{1,0:T(2,128)S(1)} %broadcast_select_fusion.2, bf16[2,8,128,128]{3,2,1,0:T(8,128)(2,1)S(1)} %bitcast.170, bf16[2,8,1024,128]{3,2,1,0:T(8,128)(2,1)} %bitcast.159), kind=kOutput, calls=%fused_computation.99 | convolution fusion | flops 545260544 | bytes 13123584 | tf_op jit(solution)/shard_map/sub | solution.py:54
  216.6 5.3 %fusion.8 = bf16[2,8,128,1024]{3,2,1,0:T(8,128)(2,1)} fusion(f32[2,8,128,1024]{3,2,1,0:T(8,128)} %get-tuple-element.36, f32[2,8,128]{2,1,0:T(8,128)S(1)} %get-tuple-element.35), kind=kLoop, calls=%fused_computation.23 | loop fusion | flops 4194304 | bytes 12591104 | tf_op jit(solution)/shard_map/convert_element_type | solution.py:56
  221.9 5.9 %multiply_reduce_fusion = (f32[2,8,128]{2,1,0:T(8,128)S(1)}, bf16[2,8,128,128]{2,3,1,0:T(8,128)(2,1)}) fusion(bf16[8,128,2,128]{1,3,2,0:T(8,128)(2,1)} %bitcast.32, bf16[2,8,128,1024]{3,2,1,0:T(8,128)(2,1)} %fusion.8, bf16[2,8,1024,128]{3,2,1,0:T(8,128)(2,1)} %bitcast.161), kind=kOutput, calls=%fused_computation.43 | convolution fusion | flops 538179584 | bytes 9445376 | tf_op jit(solution)/shard_map/hbqk,hbkd->hbqd/dot_general | solution.py:57
  227.8 6.1 %select_reduce_fusion.1 = (f32[2]{0:T(128)S(1)}, f32[2]{0:T(128)S(1)}, bf16[2,8,128,1024]{3,2,1,0:T(8,128)(2,1)S(1)}) fusion(pred[1024]{0:T(1024)(128)(4,1)S(1)} %iota_compare_fusion.5, f32[2,8,128]{2,1,0:T(8,128)S(1)} %get-tuple-element.37, bf16[2,8,1024,128]{3,2,1,0:T(8,128)(2,1)S(1)} %bitcast.162, bf16[2,8,128,128]{2,3,0,1:T(8,128)(2,1)} %bitcast.34, ...), kind=kOutput, calls=%fused_computation.13 | convolution fusion | flops 553648128 | bytes 17318928 | tf_op jit(solution)/shard_map/hbqd,hbkd->hbqk/dot_general | solution.py:65
  235.2 4.6 broadcast_multiply_fusion
  239.9 5.6 %fusion.43 = f32[2,8,1024,128]{3,2,1,0:T(8,128)} fusion(bf16[2,8,128,1024]{3,2,1,0:T(8,128)(2,1)S(1)} %copy-done.2, bf16[2,8,128,128]{2,3,0,1:T(8,128)(2,1)} %bitcast.34), kind=kOutput, calls=%fused_computation.44 | convolution fusion | flops 536870912 | bytes 13107200 | tf_op jit(solution)/shard_map/hbqk,hbqd->hbkd/dot_general | solution.py:95
  246.1 10.8 %fusion.37 = bf16[8,128,2,128]{3,0,1,2:T(8,128)(2,1)S(1)} fusion(f32[2,8,8,128,128]{4,3,2,1,0:T(8,128)} %bitcast.156, s32[8,8]{1,0:T(8,128)S(1)} %copy.182), kind=kOutput, calls=%fused_computation.41 | convolution fusion | flops 201589248 | bytes 8913152 | tf_op jit(solution)/shard_map/bjc,hbjtd->hctd/dot_general | solution.py:101
  257.6 11.0 %fusion.40 = bf16[8,128,2,128]{3,0,1,2:T(8,128)(2,1)S(1)} fusion(f32[2,8,8,128,128]{4,3,2,1,0:T(8,128)} %bitcast.155, s32[8,8]{1,0:T(8,128)S(1)} %copy.182), kind=kOutput, calls=%fused_computation.42 | convolution fusion | flops 201589248 | bytes 8913152 | tf_op jit(solution)/shard_map/bjc,hbjtd->hctd/dot_general | solution.py:107
  272.0 5.0 %all-to-all-start.4 = ((bf16[1024,3,256]{2,1,0:T(4,128)(2,1)}), bf16[1024,3,256]{2,1,0:T(4,128)(2,1)S(1)}, u32[]{:S(2)}, u32[]{:S(2)}) async-start(bf16[1024,3,256]{2,1,0:T(4,128)(2,1)} %copy.189), calls=%async_computation.4 | async-start | bytes 4194304 | tf_op jit(solution)/shard_map/all_to_all | solution.py:173
  282.2 4.7 %reduce.10 = bf16[1024,256]{1,0:T(8,128)(2,1)} reduce(bf16[1024,1,256]{2,1,0:T(2,128)(2,1)S(1)} %reshape.361, bf16[]{:T(256)} %broadcast.184), dimensions={1}, to_apply=%reshape.361.reduce_sub_computation | reduce | bytes 1048578 | tf_op jit(solution)/shard_map/reshape;reshape | solution.py:167
  288.9 37.1 %all-to-all-done.4 = bf16[1024,3,256]{2,1,0:T(4,128)(2,1)S(1)} async-done(((bf16[1024,3,256]{2,1,0:T(4,128)(2,1)}), bf16[1024,3,256]{2,1,0:T(4,128)(2,1)S(1)}, u32[]{:S(2)}, u32[]{:S(2)}) %all-to-all-start.4) | async-done | bytes 1572896 | tf_op jit(solution)/shard_map/all_to_all | solution.py:173
  334.7 6.6 %scatter_custom_fusion = bf16[384,6144]{1,0:T(8,128)(2,1)} fusion(s32[128]{0:T(128)S(1)} %get-tuple-element.27, bf16[128,6144]{1,0:T(8,128)(2,1)} %copy.192, bf16[]{:T(256)} %constant.84.clone.1), kind=kCustom, calls=%fused_computation.26 | custom fusion | bytes 4719104 | tf_op jit(solution)/shard_map/scatter | solution.py:178
  349.8 9.9 %psum.7 = f32[2,2]{0,1:T(2,128)S(1)} all-reduce(f32[2,2]{0,1:T(2,128)S(1)} %pad_maximum_fusion.1), channel_id=1, replica_groups=mesh['seq'=8,'mp'=4] {'mp'}, use_global_device_ids=true, to_apply=%region_13.14 | all-reduce | flops 4 | bytes 32 | tf_op jit(solution)/shard_map/psum | solution.py:188
  362.3 92.6 %all-to-all-done.5 = bf16[8,48,6144]{2,1,0:T(8,128)(2,1)} async-done(((bf16[8,48,6144]{2,1,0:T(8,128)(2,1)}), bf16[8,48,6144]{2,1,0:T(8,128)(2,1)}, u32[]{:S(2)}, u32[]{:S(2)}) %all-to-all-start.5) | async-done | bytes 4718624 | tf_op jit(solution)/shard_map/all_to_all | solution.py:180
  454.9 11.3 %scatter_custom_fusion.1 = bf16[385,6144]{1,0:T(8,128)(2,1)} fusion(s32[384]{0:T(512)S(1)} %fusion.61, bf16[384,6144]{1,0:T(8,128)(2,1)} %bitcast.56, bf16[]{:T(256)} %constant.84.clone.1), kind=kCustom, calls=%fused_computation.24 | custom fusion | bytes 4731392 | tf_op jit(solution)/shard_map/scatter | solution.py:185
  466.2 5.1 %slice_bitcast_fusion = bf16[1,384,6144]{2,1,0:T(8,128)(2,1)} fusion(bf16[385,6144]{1,0:T(8,128)(2,1)} %scatter_custom_fusion.1), kind=kLoop, calls=%fused_computation.17 | loop fusion | bytes 9437184 | tf_op jit(solution)/shard_map/reshape | solution.py:191
  (90 shorter events, 61.3 us)
Async XLA Ops:
  0.6 148.0 %copy-start = (f32[16,2]{0,1:T(2,128)S(1)}, f32[16,2]{0,1:T(2,128)}, u32[]{:S(2)}) copy-start(f32[16,2]{0,1:T(2,128)} %param.10) | copy-start | bytes 388
  21.7 6.5 %copy-start.6 = (s32[1,1024]{1,0:T(1,128)S(1)}, s32[1,1024]{1,0:T(1,128)}, u32[]{:S(2)}) copy-start(s32[1,1024]{1,0:T(1,128)} %param.7) | copy-start | bytes 12292
  21.7 111.8 %all-to-all-start = ((bf16[8,48,6144]{2,1,0:T(8,128)(2,1)}), bf16[8,48,6144]{2,1,0:T(8,128)(2,1)}, u32[]{:S(2)}, u32[]{:S(2)}) async-start(bf16[8,48,6144]{2,1,0:T(8,128)(2,1)} %broadcast_select_fusion), calls=%async_computation | async-start | bytes 9437184 | tf_op jit(solution)/shard_map/all_to_all | solution.py:146
  139.9 6.4 %copy-start.7 = (s32[1,8,4]{1,2,0:T(4,128)S(1)}, s32[1,8,4]{1,2,0:T(4,128)}, u32[]{:S(2)}) copy-start(s32[1,8,4]{1,2,0:T(4,128)} %param.9) | copy-start | bytes 388
  139.9 6.4 %copy-start.8 = (s32[1,8,4]{1,2,0:T(4,128)S(1)}, s32[1,8,4]{1,2,0:T(4,128)}, u32[]{:S(2)}) copy-start(s32[1,8,4]{1,2,0:T(4,128)} %param.8) | copy-start | bytes 388
  142.5 41.5 %all-to-all-start.1 = ((bf16[128,3,8,256]{0,3,1,2:T(8,128)(2,1)}), bf16[128,3,8,256]{0,3,1,2:T(8,128)(2,1)S(1)}, u32[]{:S(2)}, u32[]{:S(2)}) async-start(bf16[128,3,8,256]{0,3,1,2:T(8,128)(2,1)} %broadcast_select_fusion.1), calls=%async_computation.1 | async-start | bytes 3145728 | tf_op jit(solution)/shard_map/all_to_all | solution.py:156
  184.0 37.9 %all-to-all-start.3 = ((bf16[128,1,8,256]{0,3,1,2:T(8,128)(2,1)}), bf16[128,1,8,256]{0,3,1,2:T(8,128)(2,1)}, u32[]{:S(2)}, u32[]{:S(2)}) async-start(bf16[128,1,8,256]{0,3,1,2:T(8,128)(2,1)} %bitcast.29), calls=%async_computation.3 | async-start | bytes 1048576 | tf_op jit(solution)/shard_map/all_to_all | solution.py:157
  221.9 5.9 %copy-start.4 = (bf16[2,8,8,128,128]{4,3,2,1,0:T(8,128)(2,1)S(1)}, bf16[2,8,8,128,128]{4,3,2,1,0:T(8,128)(2,1)}, u32[]{:S(2)}) copy-start(bf16[2,8,8,128,128]{4,3,2,1,0:T(8,128)(2,1)} %copy.171) | copy-start | bytes 12582916
  227.8 6.2 %copy-start.3 = (bf16[2,8,8,128,128]{4,3,2,1,0:T(8,128)(2,1)S(1)}, bf16[2,8,8,128,128]{4,3,2,1,0:T(8,128)(2,1)}, u32[]{:S(2)}) copy-start(bf16[2,8,8,128,128]{4,3,2,1,0:T(8,128)(2,1)} %copy.169) | copy-start | bytes 12582916
  235.2 4.6 copy-start.2
  269.4 7.6 %copy-start.5 = (bf16[2,8,128,128]{2,3,1,0:T(8,128)(2,1)S(1)}, bf16[2,8,128,128]{2,3,1,0:T(8,128)(2,1)}, u32[]{:S(2)}) copy-start(bf16[2,8,128,128]{2,3,1,0:T(8,128)(2,1)} %get-tuple-element.38) | copy-start | bytes 1572868
  272.0 54.1 %all-to-all-start.4 = ((bf16[1024,3,256]{2,1,0:T(4,128)(2,1)}), bf16[1024,3,256]{2,1,0:T(4,128)(2,1)S(1)}, u32[]{:S(2)}, u32[]{:S(2)}) async-start(bf16[1024,3,256]{2,1,0:T(4,128)(2,1)} %copy.189), calls=%async_computation.4 | async-start | bytes 4194304 | tf_op jit(solution)/shard_map/all_to_all | solution.py:173
  326.1 19.0 %all-to-all-start.2 = ((bf16[8,2,16384]{2,1,0:T(2,128)(2,1)}), bf16[8,2,16384]{2,1,0:T(2,128)(2,1)S(1)}, u32[]{:S(2)}, u32[]{:S(2)}) async-start(bf16[8,2,16384]{2,1,0:T(2,128)(2,1)} %reshape.371), calls=%async_computation.2 | async-start | bytes 1048576 | tf_op jit(solution)/shard_map/all_to_all | solution.py:166
  345.1 109.9 %all-to-all-start.5 = ((bf16[8,48,6144]{2,1,0:T(8,128)(2,1)}), bf16[8,48,6144]{2,1,0:T(8,128)(2,1)}, u32[]{:S(2)}, u32[]{:S(2)}) async-start(bf16[8,48,6144]{2,1,0:T(8,128)(2,1)} %bitcast.157), calls=%async_computation.5 | async-start | bytes 9437184 | tf_op jit(solution)/shard_map/all_to_all | solution.py:180
  454.9 16.3 %copy-start.1 = (f32[16,2]{0,1:T(2,128)S(1)}, f32[16,2]{0,1:T(2,128)}, u32[]{:S(2)}) copy-start(f32[16,2]{0,1:T(2,128)} %param.10) | copy-start | bytes 388
where the time goes:
time: 481 us; the launch traced here: 472 us
  waiting for transfers between devices  271 us (56%)
  local copies, waits for them, and re-layouts  87.5 us (18%)
  matrix products  53.5 us (11%)
  starting transfers between devices  27.7 us (6%)
  other arithmetic  20.5 us (4%)
  blocking collectives  9.93 us (2%)
    all_to_all x1, waiting for transfers between devices, shards(): lax.all_to_all(outgoing, 'seq', split_axis=0, concat_axis=0, tiled=True)  102 us
    all_to_all x1, waiting for transfers between devices, shards(): lax.all_to_all(send_back, 'seq', split_axis=0, concat_axis=0, tiled=True)  92.6 us
    all_to_all x1, waiting for transfers between devices, shards(): lax.all_to_all(grad_rows, 'seq', split_axis=0, concat_axis=2, tiled=True)  37.1 us
    all_to_all x1, waiting for transfers between devices, shards(): lax.all_to_all(balanced, 'seq', split_axis=2, concat_axis=0, tiled=True)  35.3 us
    gather x1, local copies, waits for them, and re-layouts, shards(): outgoing = jnp.take(cell_rows, pick_rows, axis=0)  14.6 us
    scatter x1, local copies, waits for them, and re-layouts, shards(): jnp.zeros((slot_count + 1, features), jnp.bfloat16).at[target].set(returned)  11.3 us
    dot_general x1, matrix products, attend_both(): jnp.einsum('bjc,hbjtd->hctd', block_hot, selected_value_gradient.reshape(...  11 us
    dot_general x1, matrix products, attend_both(): jnp.einsum('bjc,hbjtd->hctd', block_hot, selected_key_gradient.reshape(pe...  10.8 us
  transfers between devices with their start and end apart: 6, of which 5 were waited for; matrix products, arithmetic and copies ran while one was open for 14% of the time, Pallas kernels for 0%

commit v1 on v0

v1 whole, which is shorter than its diff:
```python
import functools
import math

import jax
import jax.numpy as jnp
from jax import lax
from jax.experimental import pallas as pl
from jax.experimental.pallas import tpu as pltpu
from jax.sharding import PartitionSpec as P

HEADS = 16
HEAD_DIM = 128
ROW_BLOCKS = 4
VMEM_LIMIT = 56 * 1024 * 1024


def source_slots(owner_all, slot_count):
    position = jnp.arange(owner_all.shape[0], dtype=jnp.int32)
    same = owner_all[:, None] == owner_all[None, :]
    earlier = position[None, :] < position[:, None]
    return owner_all * slot_count + jnp.sum((same & earlier).astype(jnp.int32), axis=1)


def pack_kernel(slots, q_ref, k_ref, v_ref, g_ref, out_ref):
    out_ref[0, 0:slots, :] = q_ref[...]
    out_ref[0, slots : 2 * slots, :] = k_ref[...]
    out_ref[0, 2 * slots : 3 * slots, :] = v_ref[...]
    out_ref[0, 3 * slots :, :] = g_ref[...]


def pack(cells, grads, head, per_dev, num_dev):
    slots, tok = cells.shape[0], grads.shape[0]

    def part(j):
        return pl.BlockSpec((slots, HEAD_DIM), lambda d: (0, j * HEADS + d * per_dev + head))

    return pl.pallas_call(
        functools.partial(pack_kernel, slots),
        grid=(num_dev,),
        in_specs=[
            part(0),
            part(1),
            part(2),
            pl.BlockSpec((tok, HEAD_DIM), lambda d: (0, d * per_dev + head)),
        ],
        out_specs=pl.BlockSpec((1, 3 * slots + tok, HEAD_DIM), lambda d: (d, 0, 0)),
        out_shape=jax.ShapeDtypeStruct((num_dev, 3 * slots + tok, HEAD_DIM), jnp.bfloat16),
        compiler_params=pltpu.CompilerParams(vmem_limit_bytes=VMEM_LIMIT),
        cost_estimate=pl.CostEstimate(
            flops=0, bytes_accessed=4 * num_dev * (3 * slots + tok) * HEAD_DIM, transcendentals=0
        ),
    )(cells, cells, cells, grads)


def unpack_kernel(*refs):
    out_ref = refs[-1]
    for h, ref in enumerate(refs[:-1]):
        out_ref[:, h * HEAD_DIM : (h + 1) * HEAD_DIM] = ref[0]


def unpack(arrived, slots):
    per_dev, num_dev = len(arrived), arrived[0].shape[0]
    width = per_dev * HEAD_DIM
    return pl.pallas_call(
        unpack_kernel,
        grid=(num_dev, 3),
        in_specs=[pl.BlockSpec((1, slots, HEAD_DIM), lambda s, j: (s, j, 0))] * per_dev,
        out_specs=pl.BlockSpec((slots, width), lambda s, j: (0, j * num_dev + s)),
        out_shape=jax.ShapeDtypeStruct((slots, 3 * num_dev * width), jnp.bfloat16),
        compiler_params=pltpu.CompilerParams(vmem_limit_bytes=VMEM_LIMIT),
        cost_estimate=pl.CostEstimate(
            flops=0, bytes_accessed=4 * slots * 3 * num_dev * width, transcendentals=0
        ),
    )(*arrived)


def dot(a, b, dims):
    return lax.dot_general(a, b, (dims, ((), ())), preferred_element_type=jnp.float32)


def attend_kernel(
    slots, tok, sel_ref, bias_ref, in_ref, col_ref, row_ref, out_ref, sum_ref,
    cells, qkv, ksel, vsel, dkey, dval, grads,
):
    num_dev = in_ref.shape[0]
    num_blocks, num_sel = sel_ref.shape
    total = num_dev * slots
    dim = HEAD_DIM
    scaling = 1.0 / math.sqrt(dim)

    @pl.loop(0, num_dev)
    def _(o):
        start = pl.multiple_of(o * slots, slots)
        for j in range(3):
            cells[pl.ds(start, slots), j * dim : (j + 1) * dim] = in_ref[
                o, j * slots : (j + 1) * slots, :
            ]

    @pl.loop(0, num_blocks)
    def _(b):
        rows = pl.ds(pl.multiple_of(b * tok, tok), tok)
        ids = lax.broadcasted_iota(jnp.int32, (tok, total), 1)
        hot = jnp.where(ids == col_ref[rows, :], 1.0, 0.0).astype(jnp.bfloat16)
        qkv[rows, :] = dot(hot, cells[...], ((1,), (0,))).astype(jnp.bfloat16)

    dkey[...] = jnp.zeros_like(dkey)
    dval[...] = jnp.zeros_like(dval)
    sum_ref[...] = jnp.zeros_like(sum_ref)
    kind = lax.broadcasted_iota(jnp.int32, (1, num_sel * tok), 1) >= ROW_BLOCKS * tok
    offset = jnp.where(kind, bias_ref[0, 1], bias_ref[0, 0])

    @pl.loop(0, num_blocks)
    def _(b):
        rows = pl.ds(pl.multiple_of(b * tok, tok), tok)
        query = qkv[rows, 0:dim]
        grad = in_ref[b, 3 * slots :, :]
        for i in range(num_sel):
            chosen = pl.ds(pl.multiple_of(sel_ref[b, i] * tok, tok), tok)
            ksel[i * tok : (i + 1) * tok, :] = qkv[chosen, dim : 2 * dim]
            vsel[i * tok : (i + 1) * tok, :] = qkv[chosen, 2 * dim : 3 * dim]
        scores = dot(query, ksel[...], ((1,), (1,))) * scaling + offset
        exps = jnp.exp(scores - jnp.max(scores, axis=1, keepdims=True))
        probs = exps * (1.0 / jnp.sum(exps, axis=1, keepdims=True))
        low = probs.astype(jnp.bfloat16)
        result = dot(low, vsel[...], ((1,), (0,))).astype(jnp.bfloat16)
        out_ref[b, 3 * slots :, :] = result
        delta = jnp.sum(
            grad.astype(jnp.float32) * result.astype(jnp.float32), axis=1, keepdims=True
        )
        dscore = probs * (dot(grad, vsel[...], ((1,), (1,))) - delta)
        sum_ref[...] += jnp.sum(dscore.reshape(tok // 8, 8, num_sel * tok), axis=0)
        dlow = dscore.astype(jnp.bfloat16)
        grads[rows, 0:dim] = (dot(dlow, ksel[...], ((1,), (0,))) * scaling).astype(jnp.bfloat16)
        dk = dot(dlow, query, ((0,), (0,))) * scaling
        dv = dot(low, grad, ((0,), (0,)))
        for i in range(num_sel):
            chosen = pl.ds(pl.multiple_of(sel_ref[b, i] * tok, tok), tok)
            dkey[chosen, :] += dk[i * tok : (i + 1) * tok, :]
            dval[chosen, :] += dv[i * tok : (i + 1) * tok, :]

    grads[:, dim : 2 * dim] = dkey[...].astype(jnp.bfloat16)
    grads[:, 2 * dim : 3 * dim] = dval[...].astype(jnp.bfloat16)

    @pl.loop(0, num_dev)
    def _(o):
        ids = lax.broadcasted_iota(jnp.int32, (slots, num_blocks * tok), 0) + o * slots
        hot = jnp.where(ids == row_ref[...], 1.0, 0.0).astype(jnp.bfloat16)
        back = dot(hot, grads[...], ((1,), (0,))).astype(jnp.bfloat16)
        for j in range(3):
            out_ref[o, j * slots : (j + 1) * slots, :] = back[:, j * dim : (j + 1) * dim]


def attend(arrived, source, selected, bias_pair, slots, tok):
    num_dev = arrived.shape[0]
    num_sel = selected.shape[1]
    length = source.shape[0]
    vmem = pl.BlockSpec(memory_space=pltpu.VMEM)
    smem = pl.BlockSpec(memory_space=pltpu.SMEM)
    dim = HEAD_DIM
    flops = 12 * length * num_sel * tok * dim + 12 * length * num_dev * slots * dim
    return pl.pallas_call(
        functools.partial(attend_kernel, slots, tok),
        in_specs=[smem, smem, vmem, vmem, vmem],
        out_specs=[vmem, vmem],
        out_shape=[
            jax.ShapeDtypeStruct(arrived.shape, jnp.bfloat16),
            jax.ShapeDtypeStruct((8, num_sel * tok), jnp.float32),
        ],
        scratch_shapes=[
            pltpu.VMEM((num_dev * slots, 3 * dim), jnp.bfloat16),
            pltpu.VMEM((length, 3 * dim), jnp.bfloat16),
            pltpu.VMEM((num_sel * tok, dim), jnp.bfloat16),
            pltpu.VMEM((num_sel * tok, dim), jnp.bfloat16),
            pltpu.VMEM((length, dim), jnp.float32),
            pltpu.VMEM((length, dim), jnp.float32),
            pltpu.VMEM((length, 3 * dim), jnp.bfloat16),
        ],
        compiler_params=pltpu.CompilerParams(vmem_limit_bytes=VMEM_LIMIT),
        cost_estimate=pl.CostEstimate(
            flops=2 * flops,
            bytes_accessed=4 * arrived.size,
            transcendentals=length * num_sel * tok,
        ),
    )(selected, bias_pair, arrived, source[:, None], source[None, :])


def exchange(array):
    return lax.all_to_all(array, "seq", split_axis=0, concat_axis=0, tiled=True)


def shards(qkv_owned, owner, band_rows, band_cols, bias, grad_out):
    num_dev = lax.axis_size("seq")
    my_index = lax.axis_index("seq")
    slots = qkv_owned.shape[1]
    tok = grad_out.shape[1]
    per_dev = HEADS // num_dev
    cells, grads = qkv_owned[0], grad_out[0]
    arrived = [exchange(pack(cells, grads, h, per_dev, num_dev)) for h in range(per_dev)]
    source = source_slots(owner[0], slots)
    selected = jnp.concatenate([band_rows[0], band_cols[0]], axis=1)
    bias_pair = lax.dynamic_slice_in_dim(bias, my_index * per_dev, per_dev, 0)
    back, sums = [], []
    for h in range(per_dev):
        out, part = attend(arrived[h], source, selected, bias_pair[h : h + 1], slots, tok)
        back.append(exchange(out))
        sums.append(part)
    sums = jnp.stack(sums)
    bias_grad = jnp.stack(
        [
            jnp.sum(sums[:, :, : ROW_BLOCKS * tok], axis=(1, 2)),
            jnp.sum(sums[:, :, ROW_BLOCKS * tok :], axis=(1, 2)),
        ],
        axis=1,
    )
    grad_cells = unpack(back, slots)
    attended = jnp.concatenate(
        [back[h][d, 3 * slots :, :] for d in range(num_dev) for h in range(per_dev)], axis=1
    )
    return attended[None], grad_cells[None], lax.psum(bias_grad, "mp")


def solution(mesh):
    in_specs = (
        P("mp", "seq", None),
        P("mp", None),
        P("mp", None, None),
        P("mp", None, None),
        P(),
        P("mp", "seq", None),
    )
    out_specs = (P("mp", "seq", None), P("mp", "seq", None), P("seq", None))
    return jax.shard_map(shards, mesh=mesh, in_specs=in_specs, out_specs=out_specs, check_vma=False)
```

time: 481 us -> 298 us (0.62); the launches traced: 472 us -> 296 us
  waiting for transfers between devices: 271 us -> 175 us
  Pallas kernels: 0 us -> 71 us
  local copies, waits for them, and re-layouts: 87.5 us -> 18.6 us
  matrix products: 53.5 us -> 0 us
  other arithmetic: 20.5 us -> 1.91 us
  starting transfers between devices: 27.7 us -> 18.1 us
    all_to_all x6 -> x4, waiting for transfers between devices: 271 us -> 175 us  [exchange(): return lax.all_to_all(array, 'seq', split_axis=0, concat_axis=0, tiled=True)]
    pallas_call x0 -> x5, Pallas kernels: none -> 71 us  [the longest x2 44.4 us: attend(): pl.pallas_call(functools.partial(attend_kernel, slots, tok), in_specs=[sm...]
    dot_general x7 -> x0, matrix products: 45.4 us -> none  [the longest x1 11 us: attend_both(): jnp.einsum('bjc,hbjtd->hctd', block_hot, selected_value_gradient.reshape(...]
    gather x7 -> x0, local copies, waits for them, and re-layouts: 37.5 us -> none  [the longest x1 14.6 us: shards(): outgoing = jnp.take(cell_rows, pick_rows, axis=0)]
    scatter x2 -> x0, local copies, waits for them, and re-layouts: 17.8 us -> none  [the longest x1 11.3 us: shards(): jnp.zeros((slot_count + 1, features), jnp.bfloat16).at[target].set(returned)]
    unnamed x25 -> x38, local copies, waits for them, and re-layouts: 6.76 us -> 16.5 us
    all_to_all x6 -> x4, starting transfers between devices: 27.7 us -> 18.1 us  [exchange(): return lax.all_to_all(array, 'seq', split_axis=0, concat_axis=0, tiled=True)]
    another operation x7 -> x0, local copies, waits for them, and re-layouts: 8.41 us -> none  [the longest x3 5.18 us: shards(): attention_result.reshape(length, 1, group_width)]
  transfers between devices with their start and end apart: 6 -> 4, of which waited for: 5 -> 4; matrix products, arithmetic and copies ran while one was open for 14% -> 2% of each run, Pallas kernels for 0% -> 17%
where the time goes in v1:
time: 298 us; the launch traced here: 296 us
  waiting for transfers between devices  175 us (59%)
  Pallas kernels  71 us (24%)
  local copies, waits for them, and re-layouts  18.6 us (6%)
  starting transfers between devices  18.1 us (6%)
  blocking collectives  9.93 us (3%)
    all_to_all x4, waiting for transfers between devices, exchange(): return lax.all_to_all(array, 'seq', split_axis=0, concat_axis=0, tiled=True)  175 us
    pallas_call x2, Pallas kernels, attend(): pl.pallas_call(functools.partial(attend_kernel, slots, tok), in_specs=[sm...  44.4 us
    all_to_all x4, starting transfers between devices, exchange(): return lax.all_to_all(array, 'seq', split_axis=0, concat_axis=0, tiled=True)  18.1 us
    unnamed x38, local copies, waits for them, and re-layouts  16.5 us
    pallas_call x1, Pallas kernels, unpack(): pl.pallas_call(unpack_kernel, grid=(num_dev, 3), in_specs=[pl.BlockSpec((...  14.5 us
    pallas_call x2, Pallas kernels, pack(): pl.pallas_call(functools.partial(pack_kernel, slots), grid=(num_dev,), in...  12.1 us
    psum x1, blocking collectives, shards(): return (attended[None], grad_cells[None], lax.psum(bias_grad, 'mp'))  9.93 us
  transfers between devices with their start and end apart: 4, of which 4 were waited for; matrix products, arithmetic and copies ran while one was open for 2% of the time, Pallas kernels for 17%

profile of v1, /device:TPU:0, one launch (start us, length us, event | category | flops | bytes accessed | tf_op | source)
XLA Modules:
  0.0 295.7 jit_solution(17956593551352371338)
XLA Ops:
  0.6 6.0 %shard_map.85 = bf16[8,1280,128]{2,1,0:T(8,128)(2,1)} custom-call(bf16[384,6144]{1,0:T(8,128)(2,1)} %bitcast.79, bf16[384,6144]{1,0:T(8,128)(2,1)} %bitcast.80, bf16[384,6144]{1,0:T(8,128)(2,1)} %bitcast.81, bf16[128,2048]{1,0:T(8,128)(2,1)} %bitcast.86), custom_call_target="tpu_custom_call" | custom-call | bytes 5242880 | tf_op jit(solution)/shard_map/pallas_call | solution.py:37
  6.7 6.3 %all-to-all-start = ((bf16[8,1280,128]{2,1,0:T(8,128)(2,1)}), bf16[8,1280,128]{2,1,0:T(8,128)(2,1)S(1)}, u32[]{:S(2)}, u32[]{:S(2)}) async-start(bf16[8,1280,128]{2,1,0:T(8,128)(2,1)} %shard_map.85), calls=%async_computation | async-start | bytes 5242880 | tf_op jit(solution)/shard_map/all_to_all | solution.py:188
  13.0 6.1 %shard_map.87 = bf16[8,1280,128]{2,1,0:T(8,128)(2,1)} custom-call(bf16[384,6144]{1,0:T(8,128)(2,1)} %bitcast.82, bf16[384,6144]{1,0:T(8,128)(2,1)} %bitcast.83, bf16[384,6144]{1,0:T(8,128)(2,1)} %bitcast.84, bf16[128,2048]{1,0:T(8,128)(2,1)} %bitcast.87), custom_call_target="tpu_custom_call" | custom-call | bytes 5242880 | tf_op jit(solution)/shard_map/pallas_call | solution.py:37
  19.1 54.2 %all-to-all-done.in_ref = bf16[8,1280,128]{2,1,0:T(8,128)(2,1)S(1)} async-done(((bf16[8,1280,128]{2,1,0:T(8,128)(2,1)}), bf16[8,1280,128]{2,1,0:T(8,128)(2,1)S(1)}, u32[]{:S(2)}, u32[]{:S(2)}) %all-to-all-start) | async-done | bytes 2621472 | tf_op jit(solution)/shard_map/all_to_all | solution.py:188
  73.3 1.5 copy-done.3
  74.8 3.6 %all-to-all-start.2 = ((bf16[8,1280,128]{2,1,0:T(8,128)(2,1)}), bf16[8,1280,128]{2,1,0:T(8,128)(2,1)S(1)}, u32[]{:S(2)}, u32[]{:S(2)}) async-start(bf16[8,1280,128]{2,1,0:T(8,128)(2,1)} %shard_map.87), calls=%async_computation.2 | async-start | bytes 5242880 | tf_op jit(solution)/shard_map/all_to_all | solution.py:188
  79.9 1.0 copy.28.col_ref
  82.2 22.2 %shard_map.86 = (bf16[8,1280,128]{2,1,0:T(8,128)(2,1)}, f32[8,1024]{1,0:T(8,128)}) custom-call(s32[8,8]{1,0:T(8,128)} %pad_add_fusion.sel_ref, f32[1,2]{1,0:T(1,128)} %copy.32.bias_ref, bf16[8,1280,128]{2,1,0:T(8,128)(2,1)} %copy-done.3, s32[1024,1]{1,0:T(8,128)} %copy.28.col_ref, s32[1,1024]{1,0:T(1,128)} %multiply_add_fusion.row_ref), custom_call_target="tpu_custom_call" | custom-call | flops 12884901888 | bytes 5242880 | tf_op jit(solution)/shard_map/pallas_call | solution.py:161
  104.4 34.3 %all-to-all-done.2.in_ref = bf16[8,1280,128]{2,1,0:T(8,128)(2,1)S(1)} async-done(((bf16[8,1280,128]{2,1,0:T(8,128)(2,1)}), bf16[8,1280,128]{2,1,0:T(8,128)(2,1)S(1)}, u32[]{:S(2)}, u32[]{:S(2)}) %all-to-all-start.2) | async-done | bytes 2621472 | tf_op jit(solution)/shard_map/all_to_all | solution.py:188
  138.7 1.5 copy-done.2
  140.2 3.6 %all-to-all-start.1 = ((bf16[8,1280,128]{2,1,0:T(8,128)(2,1)}), bf16[8,1280,128]{2,1,0:T(8,128)(2,1)S(1)}, u32[]{:S(2)}, u32[]{:S(2)}) async-start(bf16[8,1280,128]{2,1,0:T(8,128)(2,1)} %get-tuple-element.7), calls=%async_computation.1 | async-start | bytes 5242880 | tf_op jit(solution)/shard_map/all_to_all | solution.py:188
  144.4 22.2 %shard_map.88 = (bf16[8,1280,128]{2,1,0:T(8,128)(2,1)}, f32[8,1024]{1,0:T(8,128)}) custom-call(s32[8,8]{1,0:T(8,128)} %pad_add_fusion.sel_ref, f32[1,2]{1,0:T(1,128)} %copy.33.bias_ref, bf16[8,1280,128]{2,1,0:T(8,128)(2,1)} %copy-done.2, s32[1024,1]{1,0:T(8,128)} %copy.28.col_ref, s32[1,1024]{1,0:T(1,128)} %multiply_add_fusion.row_ref), custom_call_target="tpu_custom_call" | custom-call | flops 12884901888 | bytes 5242880 | tf_op jit(solution)/shard_map/pallas_call | solution.py:161
  166.6 37.4 %all-to-all-done.1.refs_0_ = bf16[8,1280,128]{2,1,0:T(8,128)(2,1)S(1)} async-done(((bf16[8,1280,128]{2,1,0:T(8,128)(2,1)}), bf16[8,1280,128]{2,1,0:T(8,128)(2,1)S(1)}, u32[]{:S(2)}, u32[]{:S(2)}) %all-to-all-start.1) | async-done | bytes 2621472 | tf_op jit(solution)/shard_map/all_to_all | solution.py:188
  204.0 4.5 %all-to-all-start.3 = ((bf16[8,1280,128]{2,1,0:T(8,128)(2,1)}), bf16[8,1280,128]{2,1,0:T(8,128)(2,1)}, u32[]{:S(2)}, u32[]{:S(2)}) async-start(bf16[8,1280,128]{2,1,0:T(8,128)(2,1)} %get-tuple-element.8), calls=%async_computation.3 | async-start | bytes 5242880 | tf_op jit(solution)/shard_map/all_to_all | solution.py:188
  208.7 9.9 %psum.7 = f32[2,2]{0,1:T(2,128)S(1)} all-reduce(f32[2,2]{0,1:T(2,128)S(1)} %pad_maximum_fusion.1), channel_id=1, replica_groups=mesh['seq'=8,'mp'=4] {'mp'}, use_global_device_ids=true, to_apply=%region_3.0 | all-reduce | flops 4 | bytes 32 | tf_op jit(solution)/shard_map/psum | solution.py:219
  219.3 49.6 %all-to-all-done.3.refs_1_ = bf16[8,1280,128]{2,1,0:T(8,128)(2,1)} async-done(((bf16[8,1280,128]{2,1,0:T(8,128)(2,1)}), bf16[8,1280,128]{2,1,0:T(8,128)(2,1)}, u32[]{:S(2)}, u32[]{:S(2)}) %all-to-all-start.3) | async-done | bytes 2621472 | tf_op jit(solution)/shard_map/all_to_all | solution.py:188
  268.9 14.5 %shard_map.89 = bf16[384,6144]{1,0:T(8,128)(2,1)} custom-call(bf16[8,1280,128]{2,1,0:T(8,128)(2,1)} %copy-done.1, bf16[8,1280,128]{2,1,0:T(8,128)(2,1)} %all-to-all-done.3.refs_1_), custom_call_target="tpu_custom_call" | custom-call | bytes 9437184 | tf_op jit(solution)/shard_map/pallas_call | solution.py:64
  284.1 0.8 constant_dynamic-update-slice_fusion.13
  285.7 0.8 constant_dynamic-update-slice_fusion.11
  286.4 0.8 constant_dynamic-update-slice_fusion.10
  287.2 0.8 constant_dynamic-update-slice_fusion.9
  288.0 0.8 constant_dynamic-update-slice_fusion.8
  288.7 0.8 constant_dynamic-update-slice_fusion.7
  294.9 0.8 copy-done.9
  (40 shorter events, 11.0 us)
Async XLA Ops:
  0.6 77.8 %copy-start = (f32[16,2]{0,1:T(2,128)S(1)}, f32[16,2]{0,1:T(2,128)}, u32[]{:S(2)}) copy-start(f32[16,2]{0,1:T(2,128)} %param.10) | copy-start | bytes 388
  6.7 66.6 %all-to-all-start = ((bf16[8,1280,128]{2,1,0:T(8,128)(2,1)}), bf16[8,1280,128]{2,1,0:T(8,128)(2,1)S(1)}, u32[]{:S(2)}, u32[]{:S(2)}) async-start(bf16[8,1280,128]{2,1,0:T(8,128)(2,1)} %shard_map.85), calls=%async_computation | async-start | bytes 5242880 | tf_op jit(solution)/shard_map/all_to_all | solution.py:188
  19.1 60.1 %copy-start.7 = (s32[1,8,4]{1,2,0:T(4,128)S(1)}, s32[1,8,4]{1,2,0:T(4,128)}, u32[]{:S(2)}) copy-start(s32[1,8,4]{1,2,0:T(4,128)} %param.8) | copy-start | bytes 388
  19.1 60.2 %copy-start.8 = (s32[1,8,4]{1,2,0:T(4,128)S(1)}, s32[1,8,4]{1,2,0:T(4,128)}, u32[]{:S(2)}) copy-start(s32[1,8,4]{1,2,0:T(4,128)} %param.9) | copy-start | bytes 388
  19.1 60.3 %copy-start.6 = (s32[1,1024]{1,0:T(1,128)S(1)}, s32[1,1024]{1,0:T(1,128)}, u32[]{:S(2)}) copy-start(s32[1,1024]{1,0:T(1,128)} %param.7) | copy-start | bytes 12292
  73.3 1.5 copy-start.3
  74.8 63.9 %all-to-all-start.2 = ((bf16[8,1280,128]{2,1,0:T(8,128)(2,1)}), bf16[8,1280,128]{2,1,0:T(8,128)(2,1)S(1)}, u32[]{:S(2)}, u32[]{:S(2)}) async-start(bf16[8,1280,128]{2,1,0:T(8,128)(2,1)} %shard_map.87), calls=%async_computation.2 | async-start | bytes 5242880 | tf_op jit(solution)/shard_map/all_to_all | solution.py:188
  138.7 1.5 copy-start.2
  140.2 63.9 %all-to-all-start.1 = ((bf16[8,1280,128]{2,1,0:T(8,128)(2,1)}), bf16[8,1280,128]{2,1,0:T(8,128)(2,1)S(1)}, u32[]{:S(2)}, u32[]{:S(2)}) async-start(bf16[8,1280,128]{2,1,0:T(8,128)(2,1)} %get-tuple-element.7), calls=%async_computation.1 | async-start | bytes 5242880 | tf_op jit(solution)/shard_map/all_to_all | solution.py:188
  204.0 15.3 %copy-start.1 = (bf16[8,1280,128]{2,1,0:T(8,128)(2,1)}, bf16[8,1280,128]{2,1,0:T(8,128)(2,1)S(1)}, u32[]{:S(2)}) copy-start(bf16[8,1280,128]{2,1,0:T(8,128)(2,1)S(1)} %all-to-all-done.1.refs_0_) | copy-start | bytes 7864324
  204.0 4.5 %copy-start.4 = (f32[8,1024]{1,0:T(8,128)S(1)}, f32[8,1024]{1,0:T(8,128)}, u32[]{:S(2)}) copy-start(f32[8,1024]{1,0:T(8,128)} %get-tuple-element.9) | copy-start | bytes 98308
  204.0 4.6 %copy-start.5 = (f32[8,1024]{1,0:T(8,128)S(1)}, f32[8,1024]{1,0:T(8,128)}, u32[]{:S(2)}) copy-start(f32[8,1024]{1,0:T(8,128)} %get-tuple-element.10) | copy-start | bytes 98308
  204.0 64.8 %all-to-all-start.3 = ((bf16[8,1280,128]{2,1,0:T(8,128)(2,1)}), bf16[8,1280,128]{2,1,0:T(8,128)(2,1)}, u32[]{:S(2)}, u32[]{:S(2)}) async-start(bf16[8,1280,128]{2,1,0:T(8,128)(2,1)} %get-tuple-element.8), calls=%async_computation.3 | async-start | bytes 5242880 | tf_op jit(solution)/shard_map/all_to_all | solution.py:188
  294.9 0.8 copy-start.9

commit v2 on v1

--- a/solution.py
+++ b/solution.py
@@ -52,26 +52,40 @@
     )(cells, cells, cells, grads)
 
 
-def unpack_kernel(*refs):
-    out_ref = refs[-1]
-    for h, ref in enumerate(refs[:-1]):
-        out_ref[:, h * HEAD_DIM : (h + 1) * HEAD_DIM] = ref[0]
-
-
-def unpack(arrived, slots):
+def unpack_kernel(per_dev, *refs):
+    cell_parts, out_parts = refs[:per_dev], refs[per_dev : 2 * per_dev]
+    cells_ref, attended_ref = refs[2 * per_dev :]
+    for s in range(cell_parts[0].shape[0]):
+        for h in range(per_dev):
+            cols = slice((s * per_dev + h) * HEAD_DIM, (s * per_dev + h + 1) * HEAD_DIM)
+            cells_ref[:, cols] = cell_parts[h][s]
+            attended_ref[:, cols] = out_parts[h][s]
+
+
+def unpack(arrived, slots, tok):
     per_dev, num_dev = len(arrived), arrived[0].shape[0]
-    width = per_dev * HEAD_DIM
+    group = math.gcd(num_dev, 4)
+    steps = num_dev // group
+    width = group * per_dev * HEAD_DIM
+    last = 3 * slots // tok
     return pl.pallas_call(
-        unpack_kernel,
-        grid=(num_dev, 3),
-        in_specs=[pl.BlockSpec((1, slots, HEAD_DIM), lambda s, j: (s, j, 0))] * per_dev,
-        out_specs=pl.BlockSpec((slots, width), lambda s, j: (0, j * num_dev + s)),
-        out_shape=jax.ShapeDtypeStruct((slots, 3 * num_dev * width), jnp.bfloat16),
+        functools.partial(unpack_kernel, per_dev),
+        grid=(steps, 3),
+        in_specs=[pl.BlockSpec((group, slots, HEAD_DIM), lambda s, j: (s, j, 0))] * per_dev
+        + [pl.BlockSpec((group, tok, HEAD_DIM), lambda s, j: (s, last, 0))] * per_dev,
+        out_specs=[
+            pl.BlockSpec((slots, width), lambda s, j: (0, j * steps + s)),
+            pl.BlockSpec((tok, width), lambda s, j: (0, s)),
+        ],
+        out_shape=[
+            jax.ShapeDtypeStruct((slots, 3 * steps * width), jnp.bfloat16),
+            jax.ShapeDtypeStruct((tok, steps * width), jnp.bfloat16),
+        ],
         compiler_params=pltpu.CompilerParams(vmem_limit_bytes=VMEM_LIMIT),
         cost_estimate=pl.CostEstimate(
-            flops=0, bytes_accessed=4 * slots * 3 * num_dev * width, transcendentals=0
+            flops=0, bytes_accessed=4 * (3 * slots + tok) * steps * width, transcendentals=0
         ),
-    )(*arrived)
+    )(*arrived, *arrived)
 
 
 def dot(a, b, dims):
@@ -212,10 +226,7 @@
         ],
         axis=1,
     )
-    grad_cells = unpack(back, slots)
-    attended = jnp.concatenate(
-        [back[h][d, 3 * slots :, :] for d in range(num_dev) for h in range(per_dev)], axis=1
-    )
+    grad_cells, attended = unpack(back, slots, tok)
     return attended[None], grad_cells[None], lax.psum(bias_grad, "mp")
 
 

time: 298 us -> 278 us (0.933)
  local copies, waits for them, and re-layouts: 18.6 us -> 7.71 us
  Pallas kernels: 71 us -> 63.4 us
    unnamed x38 -> x21, local copies, waits for them, and re-layouts: 16.5 us -> 6.37 us
    pallas_call x1, Pallas kernels: 14.5 us -> 6.89 us  [unpack(): pl.pallas_call(functools.partial(unpack_kernel, per_dev), grid=(steps, 3)...]
  transfers between devices with their start and end apart: 4 -> 4, of which waited for: 4 -> 4; matrix products, arithmetic and copies ran while one was open for 2% -> 2% of each run, Pallas kernels for 17% -> 18%
where the time goes in v2:
time: 278 us; the launch traced here: 277 us
  waiting for transfers between devices  176 us (63%)
  Pallas kernels  63.4 us (23%)
  starting transfers between devices  18 us (6%)
  blocking collectives  9.93 us (4%)
  local copies, waits for them, and re-layouts  7.71 us (3%)
    all_to_all x4, waiting for transfers between devices, exchange(): return lax.all_to_all(array, 'seq', split_axis=0, concat_axis=0, tiled=True)  176 us
    pallas_call x2, Pallas kernels, attend(): pl.pallas_call(functools.partial(attend_kernel, slots, tok), in_specs=[sm...  44.4 us
    all_to_all x4, starting transfers between devices, exchange(): return lax.all_to_all(array, 'seq', split_axis=0, concat_axis=0, tiled=True)  18 us
    pallas_call x2, Pallas kernels, pack(): pl.pallas_call(functools.partial(pack_kernel, slots), grid=(num_dev,), in...  12.1 us
    psum x1, blocking collectives, shards(): return (attended[None], grad_cells[None], lax.psum(bias_grad, 'mp'))  9.93 us
    pallas_call x1, Pallas kernels, unpack(): pl.pallas_call(functools.partial(unpack_kernel, per_dev), grid=(steps, 3)...  6.89 us
    unnamed x21, local copies, waits for them, and re-layouts  6.37 us
  transfers between devices with their start and end apart: 4, of which 4 were waited for; matrix products, arithmetic and copies ran while one was open for 2% of the time, Pallas kernels for 18%

profile of v2, /device:TPU:0, one launch (start us, length us, event | category | flops | bytes accessed | tf_op | source)
XLA Modules:
  0.0 277.2 jit_solution(3960898813024886837)
XLA Ops:
  0.6 6.1 %shard_map.87 = bf16[8,1280,128]{2,1,0:T(8,128)(2,1)} custom-call(bf16[384,6144]{1,0:T(8,128)(2,1)} %bitcast.15, bf16[384,6144]{1,0:T(8,128)(2,1)} %bitcast.16, bf16[384,6144]{1,0:T(8,128)(2,1)} %bitcast.17, bf16[128,2048]{1,0:T(8,128)(2,1)} %bitcast.21), custom_call_target="tpu_custom_call" | custom-call | bytes 5242880 | tf_op jit(solution)/shard_map/pallas_call | solution.py:37
  6.7 6.3 %all-to-all-start.2 = ((bf16[8,1280,128]{2,1,0:T(8,128)(2,1)}), bf16[8,1280,128]{2,1,0:T(8,128)(2,1)S(1)}, u32[]{:S(2)}, u32[]{:S(2)}) async-start(bf16[8,1280,128]{2,1,0:T(8,128)(2,1)} %shard_map.87), calls=%async_computation.2 | async-start | bytes 5242880 | tf_op jit(solution)/shard_map/all_to_all | solution.py:202
  13.0 6.0 %shard_map.85 = bf16[8,1280,128]{2,1,0:T(8,128)(2,1)} custom-call(bf16[384,6144]{1,0:T(8,128)(2,1)} %bitcast.18, bf16[384,6144]{1,0:T(8,128)(2,1)} %bitcast.19, bf16[384,6144]{1,0:T(8,128)(2,1)} %bitcast.20, bf16[128,2048]{1,0:T(8,128)(2,1)} %bitcast.22), custom_call_target="tpu_custom_call" | custom-call | bytes 5242880 | tf_op jit(solution)/shard_map/pallas_call | solution.py:37
  19.1 54.3 %all-to-all-done.2.in_ref = bf16[8,1280,128]{2,1,0:T(8,128)(2,1)S(1)} async-done(((bf16[8,1280,128]{2,1,0:T(8,128)(2,1)}), bf16[8,1280,128]{2,1,0:T(8,128)(2,1)S(1)}, u32[]{:S(2)}, u32[]{:S(2)}) %all-to-all-start.2) | async-done | bytes 2621472 | tf_op jit(solution)/shard_map/all_to_all | solution.py:202
  73.3 1.5 copy-done.3
  74.9 3.6 %all-to-all-start = ((bf16[8,1280,128]{2,1,0:T(8,128)(2,1)}), bf16[8,1280,128]{2,1,0:T(8,128)(2,1)S(1)}, u32[]{:S(2)}, u32[]{:S(2)}) async-start(bf16[8,1280,128]{2,1,0:T(8,128)(2,1)} %shard_map.85), calls=%async_computation | async-start | bytes 5242880 | tf_op jit(solution)/shard_map/all_to_all | solution.py:202
  78.7 0.6 copy.33.bias_ref
  79.4 0.5 convert_reduce_fusion
  80.0 1.0 copy.28.col_ref
  81.0 0.7 pad_add_fusion.sel_ref
  81.7 0.6 multiply_add_fusion.row_ref
  82.3 22.2 %shard_map.88 = (bf16[8,1280,128]{2,1,0:T(8,128)(2,1)}, f32[8,1024]{1,0:T(8,128)}) custom-call(s32[8,8]{1,0:T(8,128)} %pad_add_fusion.sel_ref, f32[1,2]{1,0:T(1,128)} %copy.33.bias_ref, bf16[8,1280,128]{2,1,0:T(8,128)(2,1)} %copy-done.3, s32[1024,1]{1,0:T(8,128)} %copy.28.col_ref, s32[1,1024]{1,0:T(1,128)} %multiply_add_fusion.row_ref), custom_call_target="tpu_custom_call" | custom-call | flops 12884901888 | bytes 5242880 | tf_op jit(solution)/shard_map/pallas_call | solution.py:175
  104.5 34.2 %all-to-all-done.in_ref = bf16[8,1280,128]{2,1,0:T(8,128)(2,1)S(1)} async-done(((bf16[8,1280,128]{2,1,0:T(8,128)(2,1)}), bf16[8,1280,128]{2,1,0:T(8,128)(2,1)S(1)}, u32[]{:S(2)}, u32[]{:S(2)}) %all-to-all-start) | async-done | bytes 2621472 | tf_op jit(solution)/shard_map/all_to_all | solution.py:202
  138.7 1.5 copy-done.2
  140.2 3.6 %all-to-all-start.3 = ((bf16[8,1280,128]{2,1,0:T(8,128)(2,1)}), bf16[8,1280,128]{2,1,0:T(8,128)(2,1)S(1)}, u32[]{:S(2)}, u32[]{:S(2)}) async-start(bf16[8,1280,128]{2,1,0:T(8,128)(2,1)} %get-tuple-element.10), calls=%async_computation.3 | async-start | bytes 5242880 | tf_op jit(solution)/shard_map/all_to_all | solution.py:202
  143.8 0.6 copy.32.bias_ref
  144.4 22.2 %shard_map.86 = (bf16[8,1280,128]{2,1,0:T(8,128)(2,1)}, f32[8,1024]{1,0:T(8,128)}) custom-call(s32[8,8]{1,0:T(8,128)} %pad_add_fusion.sel_ref, f32[1,2]{1,0:T(1,128)} %copy.32.bias_ref, bf16[8,1280,128]{2,1,0:T(8,128)(2,1)} %copy-done.2, s32[1024,1]{1,0:T(8,128)} %copy.28.col_ref, s32[1,1024]{1,0:T(1,128)} %multiply_add_fusion.row_ref), custom_call_target="tpu_custom_call" | custom-call | flops 12884901888 | bytes 5242880 | tf_op jit(solution)/shard_map/pallas_call | solution.py:175
  166.7 37.4 %all-to-all-done.3.refs_1_.refs_3_ = bf16[8,1280,128]{2,1,0:T(8,128)(2,1)S(1)} async-done(((bf16[8,1280,128]{2,1,0:T(8,128)(2,1)}), bf16[8,1280,128]{2,1,0:T(8,128)(2,1)S(1)}, u32[]{:S(2)}, u32[]{:S(2)}) %all-to-all-start.3) | async-done | bytes 2621472 | tf_op jit(solution)/shard_map/all_to_all | solution.py:202
  204.1 1.5 copy-done.1
  205.6 4.4 %all-to-all-start.1 = ((bf16[8,1280,128]{2,1,0:T(8,128)(2,1)}), bf16[8,1280,128]{2,1,0:T(8,128)(2,1)}, u32[]{:S(2)}, u32[]{:S(2)}) async-start(bf16[8,1280,128]{2,1,0:T(8,128)(2,1)} %get-tuple-element.9), calls=%async_computation.1 | async-start | bytes 5242880 | tf_op jit(solution)/shard_map/all_to_all | solution.py:202
  210.1 9.9 %psum.7 = f32[2,2]{0,1:T(2,128)S(1)} all-reduce(f32[2,2]{0,1:T(2,128)S(1)} %pad_maximum_fusion.1), channel_id=1, replica_groups=mesh['seq'=8,'mp'=4] {'mp'}, use_global_device_ids=true, to_apply=%region_3.0 | all-reduce | flops 4 | bytes 32 | tf_op jit(solution)/shard_map/psum | solution.py:230
  220.0 0.7 copy.30
  220.7 49.6 %all-to-all-done.1.refs_0_.refs_2_ = bf16[8,1280,128]{2,1,0:T(8,128)(2,1)} async-done(((bf16[8,1280,128]{2,1,0:T(8,128)(2,1)}), bf16[8,1280,128]{2,1,0:T(8,128)(2,1)}, u32[]{:S(2)}, u32[]{:S(2)}) %all-to-all-start.1) | async-done | bytes 2621472 | tf_op jit(solution)/shard_map/all_to_all | solution.py:202
  270.3 6.9 %shard_map.89 = (bf16[384,6144]{1,0:T(8,128)(2,1)}, bf16[128,2048]{1,0:T(8,128)(2,1)}) custom-call(bf16[8,1280,128]{2,1,0:T(8,128)(2,1)} %all-to-all-done.1.refs_0_.refs_2_, bf16[8,1280,128]{2,1,0:T(8,128)(2,1)} %copy-done.1, bf16[8,1280,128]{2,1,0:T(8,128)(2,1)} %all-to-all-done.1.refs_0_.refs_2_, bf16[8,1280,128]{2,1,0:T(8,128)(2,1)} %copy-done.1), custom_call_target="tpu_custom_call" | custom-call | bytes 10485760 | tf_op jit(solution)/shard_map/pallas_call | solution.py:71
  (22 shorter events, 0.5 us)
Async XLA Ops:
  0.6 77.9 %copy-start = (f32[16,2]{0,1:T(2,128)S(1)}, f32[16,2]{0,1:T(2,128)}, u32[]{:S(2)}) copy-start(f32[16,2]{0,1:T(2,128)} %param.10) | copy-start | bytes 388
  6.7 66.6 %all-to-all-start.2 = ((bf16[8,1280,128]{2,1,0:T(8,128)(2,1)}), bf16[8,1280,128]{2,1,0:T(8,128)(2,1)S(1)}, u32[]{:S(2)}, u32[]{:S(2)}) async-start(bf16[8,1280,128]{2,1,0:T(8,128)(2,1)} %shard_map.87), calls=%async_computation.2 | async-start | bytes 5242880 | tf_op jit(solution)/shard_map/all_to_all | solution.py:202
  19.1 60.2 %copy-start.7 = (s32[1,8,4]{1,2,0:T(4,128)S(1)}, s32[1,8,4]{1,2,0:T(4,128)}, u32[]{:S(2)}) copy-start(s32[1,8,4]{1,2,0:T(4,128)} %param.8) | copy-start | bytes 388
  19.1 60.3 %copy-start.8 = (s32[1,8,4]{1,2,0:T(4,128)S(1)}, s32[1,8,4]{1,2,0:T(4,128)}, u32[]{:S(2)}) copy-start(s32[1,8,4]{1,2,0:T(4,128)} %param.9) | copy-start | bytes 388
  19.1 60.4 %copy-start.6 = (s32[1,1024]{1,0:T(1,128)S(1)}, s32[1,1024]{1,0:T(1,128)}, u32[]{:S(2)}) copy-start(s32[1,1024]{1,0:T(1,128)} %param.7) | copy-start | bytes 12292
  73.3 1.5 copy-start.3
  74.9 63.9 %all-to-all-start = ((bf16[8,1280,128]{2,1,0:T(8,128)(2,1)}), bf16[8,1280,128]{2,1,0:T(8,128)(2,1)S(1)}, u32[]{:S(2)}, u32[]{:S(2)}) async-start(bf16[8,1280,128]{2,1,0:T(8,128)(2,1)} %shard_map.85), calls=%async_computation | async-start | bytes 5242880 | tf_op jit(solution)/shard_map/all_to_all | solution.py:202
  138.7 1.5 copy-start.2
  140.2 63.9 %all-to-all-start.3 = ((bf16[8,1280,128]{2,1,0:T(8,128)(2,1)}), bf16[8,1280,128]{2,1,0:T(8,128)(2,1)S(1)}, u32[]{:S(2)}, u32[]{:S(2)}) async-start(bf16[8,1280,128]{2,1,0:T(8,128)(2,1)} %get-tuple-element.10), calls=%async_computation.3 | async-start | bytes 5242880 | tf_op jit(solution)/shard_map/all_to_all | solution.py:202
  204.1 1.5 copy-start.1
  204.1 5.9 %copy-start.4 = (f32[8,1024]{1,0:T(8,128)S(1)}, f32[8,1024]{1,0:T(8,128)}, u32[]{:S(2)}) copy-start(f32[8,1024]{1,0:T(8,128)} %get-tuple-element.14) | copy-start | bytes 98308
  204.1 5.9 %copy-start.5 = (f32[8,1024]{1,0:T(8,128)S(1)}, f32[8,1024]{1,0:T(8,128)}, u32[]{:S(2)}) copy-start(f32[8,1024]{1,0:T(8,128)} %get-tuple-element.13) | copy-start | bytes 98308
  205.6 64.7 %all-to-all-start.1 = ((bf16[8,1280,128]{2,1,0:T(8,128)(2,1)}), bf16[8,1280,128]{2,1,0:T(8,128)(2,1)}, u32[]{:S(2)}, u32[]{:S(2)}) async-start(bf16[8,1280,128]{2,1,0:T(8,128)(2,1)} %get-tuple-element.9), calls=%async_computation.1 | async-start | bytes 5242880 | tf_op jit(solution)/shard_map/all_to_all | solution.py:202

commit v3 on v2

--- a/solution.py
+++ b/solution.py
@@ -21,35 +21,42 @@
     return owner_all * slot_count + jnp.sum((same & earlier).astype(jnp.int32), axis=1)
 
 
-def pack_kernel(slots, q_ref, k_ref, v_ref, g_ref, out_ref):
-    out_ref[0, 0:slots, :] = q_ref[...]
-    out_ref[0, slots : 2 * slots, :] = k_ref[...]
-    out_ref[0, 2 * slots : 3 * slots, :] = v_ref[...]
-    out_ref[0, 3 * slots :, :] = g_ref[...]
+def pack_kernel(slots, per_dev, head, cells_ref, grads_ref, out_ref, sems):
+    num_dev = out_ref.shape[0]
+    copies = []
+    for d in range(num_dev):
+        for j in range(4):
+            col = d * per_dev + head
+            if j < 3:
+                col += j * HEADS
+                source, rows = cells_ref, pl.ds(j * slots, slots)
+            else:
+                source, rows = grads_ref, pl.ds(3 * slots, grads_ref.shape[0])
+            copies.append(
+                pltpu.make_async_copy(
+                    source.at[:, pl.ds(col * HEAD_DIM, HEAD_DIM)], out_ref.at[d, rows], sems.at[d, j]
+                )
+            )
+    for copy in copies:
+        copy.start()
+    for copy in copies:
+        copy.wait()
 
 
 def pack(cells, grads, head, per_dev, num_dev):
     slots, tok = cells.shape[0], grads.shape[0]
-
-    def part(j):
-        return pl.BlockSpec((slots, HEAD_DIM), lambda d: (0, j * HEADS + d * per_dev + head))
-
+    hbm = pl.BlockSpec(memory_space=pl.ANY)
     return pl.pallas_call(
-        functools.partial(pack_kernel, slots),
-        grid=(num_dev,),
-        in_specs=[
-            part(0),
-            part(1),
-            part(2),
-            pl.BlockSpec((tok, HEAD_DIM), lambda d: (0, d * per_dev + head)),
-        ],
-        out_specs=pl.BlockSpec((1, 3 * slots + tok, HEAD_DIM), lambda d: (d, 0, 0)),
+        functools.partial(pack_kernel, slots, per_dev, head),
+        in_specs=[hbm, hbm],
+        out_specs=hbm,
         out_shape=jax.ShapeDtypeStruct((num_dev, 3 * slots + tok, HEAD_DIM), jnp.bfloat16),
+        scratch_shapes=[pltpu.SemaphoreType.DMA((num_dev, 4))],
         compiler_params=pltpu.CompilerParams(vmem_limit_bytes=VMEM_LIMIT),
         cost_estimate=pl.CostEstimate(
             flops=0, bytes_accessed=4 * num_dev * (3 * slots + tok) * HEAD_DIM, transcendentals=0
         ),
-    )(cells, cells, cells, grads)
+    )(cells, grads)
 
 
 def unpack_kernel(per_dev, *refs):

time: 278 us -> 375 us (1.35)
  Pallas kernels: 63.4 us -> 213 us
  waiting for transfers between devices: 176 us -> 121 us
    pallas_call x2, Pallas kernels: 12.1 us -> 162 us  [pack(): pl.pallas_call(functools.partial(pack_kernel, slots, per_dev, head), in_s...]
    all_to_all x4, waiting for transfers between devices: 176 us -> 121 us  [exchange(): return lax.all_to_all(array, 'seq', split_axis=0, concat_axis=0, tiled=True)]
  transfers between devices with their start and end apart: 4 -> 4, of which waited for: 4 -> 3; matrix products, arithmetic and copies ran while one was open for 2% -> 1% of each run, Pallas kernels for 18% -> 33%
where the time goes in v3:
time: 375 us; the launch traced here: 374 us
  Pallas kernels  213 us (57%)
  waiting for transfers between devices  121 us (32%)
  starting transfers between devices  19.5 us (5%)
  blocking collectives  9.93 us (3%)
  local copies, waits for them, and re-layouts  7.71 us (2%)
    pallas_call x2, Pallas kernels, pack(): pl.pallas_call(functools.partial(pack_kernel, slots, per_dev, head), in_s...  162 us
    all_to_all x4, waiting for transfers between devices, exchange(): return lax.all_to_all(array, 'seq', split_axis=0, concat_axis=0, tiled=True)  121 us
    pallas_call x2, Pallas kernels, attend(): pl.pallas_call(functools.partial(attend_kernel, slots, tok), in_specs=[sm...  44.4 us
    all_to_all x4, starting transfers between devices, exchange(): return lax.all_to_all(array, 'seq', split_axis=0, concat_axis=0, tiled=True)  19.5 us
    psum x1, blocking collectives, shards(): return (attended[None], grad_cells[None], lax.psum(bias_grad, 'mp'))  9.93 us
  transfers between devices with their start and end apart: 4, of which 3 were waited for; matrix products, arithmetic and copies ran while one was open for 1% of the time, Pallas kernels for 33%

profile of v3, /device:TPU:0, one launch (start us, length us, event | category | flops | bytes accessed | tf_op | source)
XLA Modules:
  0.0 374.0 jit_solution(14835577467942594336)
XLA Ops:
  0.6 80.8 %shard_map.87 = bf16[8,1280,128]{2,1,0:T(8,128)(2,1)} custom-call(bf16[384,6144]{1,0:T(8,128)(2,1)} %bitcast.15, bf16[128,2048]{1,0:T(8,128)(2,1)} %bitcast.17), custom_call_target="tpu_custom_call" | custom-call | bytes 5242880 | tf_op jit(solution)/shard_map/pallas_call | solution.py:49
  81.5 6.3 %all-to-all-start.2 = ((bf16[8,1280,128]{2,1,0:T(8,128)(2,1)}), bf16[8,1280,128]{2,1,0:T(8,128)(2,1)S(1)}, u32[]{:S(2)}, u32[]{:S(2)}) async-start(bf16[8,1280,128]{2,1,0:T(8,128)(2,1)} %shard_map.87), calls=%async_computation.2 | async-start | bytes 5242880 | tf_op jit(solution)/shard_map/all_to_all | solution.py:209
  87.8 80.8 %shard_map.85 = bf16[8,1280,128]{2,1,0:T(8,128)(2,1)} custom-call(bf16[384,6144]{1,0:T(8,128)(2,1)} %bitcast.16, bf16[128,2048]{1,0:T(8,128)(2,1)} %bitcast.18), custom_call_target="tpu_custom_call" | custom-call | bytes 5242880 | tf_op jit(solution)/shard_map/pallas_call | solution.py:49
  168.7 1.5 copy-done.3
  170.2 5.1 %all-to-all-start = ((bf16[8,1280,128]{2,1,0:T(8,128)(2,1)}), bf16[8,1280,128]{2,1,0:T(8,128)(2,1)S(1)}, u32[]{:S(2)}, u32[]{:S(2)}) async-start(bf16[8,1280,128]{2,1,0:T(8,128)(2,1)} %shard_map.85), calls=%async_computation | async-start | bytes 5242880 | tf_op jit(solution)/shard_map/all_to_all | solution.py:209
  175.4 0.6 copy.33.bias_ref
  176.2 0.5 convert_reduce_fusion
  176.7 1.0 copy.28.col_ref
  177.8 0.7 pad_add_fusion.sel_ref
  178.4 0.6 multiply_add_fusion.row_ref
  179.0 22.2 %shard_map.88 = (bf16[8,1280,128]{2,1,0:T(8,128)(2,1)}, f32[8,1024]{1,0:T(8,128)}) custom-call(s32[8,8]{1,0:T(8,128)} %pad_add_fusion.sel_ref, f32[1,2]{1,0:T(1,128)} %copy.33.bias_ref, bf16[8,1280,128]{2,1,0:T(8,128)(2,1)} %copy-done.3, s32[1024,1]{1,0:T(8,128)} %copy.28.col_ref, s32[1,1024]{1,0:T(1,128)} %multiply_add_fusion.row_ref), custom_call_target="tpu_custom_call" | custom-call | flops 12884901888 | bytes 5242880 | tf_op jit(solution)/shard_map/pallas_call | solution.py:182
  201.2 34.3 %all-to-all-done.in_ref = bf16[8,1280,128]{2,1,0:T(8,128)(2,1)S(1)} async-done(((bf16[8,1280,128]{2,1,0:T(8,128)(2,1)}), bf16[8,1280,128]{2,1,0:T(8,128)(2,1)S(1)}, u32[]{:S(2)}, u32[]{:S(2)}) %all-to-all-start) | async-done | bytes 2621472 | tf_op jit(solution)/shard_map/all_to_all | solution.py:209
  235.6 1.5 copy-done.2
  237.1 3.6 all-to-all-start.3
  240.7 0.6 copy.32.bias_ref
  241.3 22.2 %shard_map.86 = (bf16[8,1280,128]{2,1,0:T(8,128)(2,1)}, f32[8,1024]{1,0:T(8,128)}) custom-call(s32[8,8]{1,0:T(8,128)} %pad_add_fusion.sel_ref, f32[1,2]{1,0:T(1,128)} %copy.32.bias_ref, bf16[8,1280,128]{2,1,0:T(8,128)(2,1)} %copy-done.2, s32[1024,1]{1,0:T(8,128)} %copy.28.col_ref, s32[1,1024]{1,0:T(1,128)} %multiply_add_fusion.row_ref), custom_call_target="tpu_custom_call" | custom-call | flops 12884901888 | bytes 5242880 | tf_op jit(solution)/shard_map/pallas_call | solution.py:182
  263.5 37.4 %all-to-all-done.3.refs_1_.refs_3_ = bf16[8,1280,128]{2,1,0:T(8,128)(2,1)S(1)} async-done(((bf16[8,1280,128]{2,1,0:T(8,128)(2,1)}), bf16[8,1280,128]{2,1,0:T(8,128)(2,1)S(1)}, u32[]{:S(2)}, u32[]{:S(2)}) %all-to-all-start.3) | async-done | bytes 2621472 | tf_op jit(solution)/shard_map/all_to_all | solution.py:209
  300.9 1.5 copy-done.1
  302.4 4.4 %all-to-all-start.1 = ((bf16[8,1280,128]{2,1,0:T(8,128)(2,1)}), bf16[8,1280,128]{2,1,0:T(8,128)(2,1)}, u32[]{:S(2)}, u32[]{:S(2)}) async-start(bf16[8,1280,128]{2,1,0:T(8,128)(2,1)} %get-tuple-element.9), calls=%async_computation.1 | async-start | bytes 5242880 | tf_op jit(solution)/shard_map/all_to_all | solution.py:209
  306.8 0.1 fusion.2
  307.0 9.9 %psum.7 = f32[2,2]{0,1:T(2,128)S(1)} all-reduce(f32[2,2]{0,1:T(2,128)S(1)} %pad_maximum_fusion.1), channel_id=1, replica_groups=mesh['seq'=8,'mp'=4] {'mp'}, use_global_device_ids=true, to_apply=%region_3.0 | all-reduce | flops 4 | bytes 32 | tf_op jit(solution)/shard_map/psum | solution.py:237
  316.9 0.7 copy.30
  317.5 49.6 %all-to-all-done.1.refs_0_.refs_2_ = bf16[8,1280,128]{2,1,0:T(8,128)(2,1)} async-done(((bf16[8,1280,128]{2,1,0:T(8,128)(2,1)}), bf16[8,1280,128]{2,1,0:T(8,128)(2,1)}, u32[]{:S(2)}, u32[]{:S(2)}) %all-to-all-start.1) | async-done | bytes 2621472 | tf_op jit(solution)/shard_map/all_to_all | solution.py:209
  367.1 6.9 %shard_map.89 = (bf16[384,6144]{1,0:T(8,128)(2,1)}, bf16[128,2048]{1,0:T(8,128)(2,1)}) custom-call(bf16[8,1280,128]{2,1,0:T(8,128)(2,1)} %all-to-all-done.1.refs_0_.refs_2_, bf16[8,1280,128]{2,1,0:T(8,128)(2,1)} %copy-done.1, bf16[8,1280,128]{2,1,0:T(8,128)(2,1)} %all-to-all-done.1.refs_0_.refs_2_, bf16[8,1280,128]{2,1,0:T(8,128)(2,1)} %copy-done.1), custom_call_target="tpu_custom_call" | custom-call | bytes 10485760 | tf_op jit(solution)/shard_map/pallas_call | solution.py:78
  (22 shorter events, 0.4 us)
Async XLA Ops:
  0.6 174.6 %copy-start = (f32[16,2]{0,1:T(2,128)S(1)}, f32[16,2]{0,1:T(2,128)}, u32[]{:S(2)}) copy-start(f32[16,2]{0,1:T(2,128)} %param.10) | copy-start | bytes 388
  81.5 87.2 %all-to-all-start.2 = ((bf16[8,1280,128]{2,1,0:T(8,128)(2,1)}), bf16[8,1280,128]{2,1,0:T(8,128)(2,1)S(1)}, u32[]{:S(2)}, u32[]{:S(2)}) async-start(bf16[8,1280,128]{2,1,0:T(8,128)(2,1)} %shard_map.87), calls=%async_computation.2 | async-start | bytes 5242880 | tf_op jit(solution)/shard_map/all_to_all | solution.py:209
  168.6 7.4 %copy-start.7 = (s32[1,8,4]{1,2,0:T(4,128)S(1)}, s32[1,8,4]{1,2,0:T(4,128)}, u32[]{:S(2)}) copy-start(s32[1,8,4]{1,2,0:T(4,128)} %param.8) | copy-start | bytes 388
  168.6 7.5 %copy-start.8 = (s32[1,8,4]{1,2,0:T(4,128)S(1)}, s32[1,8,4]{1,2,0:T(4,128)}, u32[]{:S(2)}) copy-start(s32[1,8,4]{1,2,0:T(4,128)} %param.9) | copy-start | bytes 388
  168.6 7.6 %copy-start.6 = (s32[1,1024]{1,0:T(1,128)S(1)}, s32[1,1024]{1,0:T(1,128)}, u32[]{:S(2)}) copy-start(s32[1,1024]{1,0:T(1,128)} %param.7) | copy-start | bytes 12292
  168.6 1.5 copy-start.3
  170.2 65.4 %all-to-all-start = ((bf16[8,1280,128]{2,1,0:T(8,128)(2,1)}), bf16[8,1280,128]{2,1,0:T(8,128)(2,1)S(1)}, u32[]{:S(2)}, u32[]{:S(2)}) async-start(bf16[8,1280,128]{2,1,0:T(8,128)(2,1)} %shard_map.85), calls=%async_computation | async-start | bytes 5242880 | tf_op jit(solution)/shard_map/all_to_all | solution.py:209
  235.6 1.5 copy-start.2
  237.1 63.9 %all-to-all-start.3 = ((bf16[8,1280,128]{2,1,0:T(8,128)(2,1)}), bf16[8,1280,128]{2,1,0:T(8,128)(2,1)S(1)}, u32[]{:S(2)}, u32[]{:S(2)}) async-start(bf16[8,1280,128]{2,1,0:T(8,128)(2,1)} %get-tuple-element.10), calls=%async_computation.3 | async-start | bytes 5242880 | tf_op jit(solution)/shard_map/all_to_all | solution.py:209
  300.9 1.5 copy-start.1
  300.9 5.9 %copy-start.4 = (f32[8,1024]{1,0:T(8,128)S(1)}, f32[8,1024]{1,0:T(8,128)}, u32[]{:S(2)}) copy-start(f32[8,1024]{1,0:T(8,128)} %get-tuple-element.14) | copy-start | bytes 98308
  300.9 5.9 %copy-start.5 = (f32[8,1024]{1,0:T(8,128)S(1)}, f32[8,1024]{1,0:T(8,128)}, u32[]{:S(2)}) copy-start(f32[8,1024]{1,0:T(8,128)} %get-tuple-element.13) | copy-start | bytes 98308
  302.4 64.7 %all-to-all-start.1 = ((bf16[8,1280,128]{2,1,0:T(8,128)(2,1)}), bf16[8,1280,128]{2,1,0:T(8,128)(2,1)}, u32[]{:S(2)}, u32[]{:S(2)}) async-start(bf16[8,1280,128]{2,1,0:T(8,128)(2,1)} %get-tuple-element.9), calls=%async_computation.1 | async-start | bytes 5242880 | tf_op jit(solution)/shard_map/all_to_all | solution.py:209
